TPU v7x, 32 devices: a whole 2x2x4 slice. The times are simulated.
32 devices in a mesh: node: 4 (over y, x), local: 8 (over z, core).
Axes of the slice: x: 2, y: 2, z: 4, core: 2. Of those that a mesh axis runs over, the one named last changes fastest.
Arguments:
- grads: bfloat16 [4, 8, 2, 64, 14848], P('node', 'local'), may hold values from -0.29882812 to 0.29882812
- first_scales: bfloat16 [4, 8, 14848], P('node', 'local'), may hold values from 0.00390625 to 0.03125, as said below
- second_scales: bfloat16 [4, 14848], P('node', 'local'), may hold values from 0.00390625 to 0.015625, as said below
- param: float32 [8, 4, 464, 128], P('local', 'node'), may hold values from -6 to 6
- first_moment: float32 [8, 4, 464, 128], P('local', 'node'), may hold values from -3 to 3
- second_moment: float32 [8, 4, 464, 128], P('local', 'node'), may hold values from 0.01 to 1
Outputs:
- grad_sum: float32 [8, 4, 464, 128], P('local', 'node')
- new_param: float32 [8, 4, 464, 128], P('local', 'node')
- new_first: float32 [8, 4, 464, 128], P('local', 'node')
- new_second: float32 [8, 4, 464, 128], P('local', 'node')
Inputs may be any that keep to these rules, and one draw needn't show every extreme that they name: `first_scales`: every entry is a power of two. `second_scales`: every entry is a power of two.
All inputs are finite; a program needn't handle non-finite values.
Results may differ from a plain program's by a relative error of at most 0.0014.
Values may be sent and summed in bfloat16 or wider, within the bound.
A program may use at most 64 MiB of HBM per device.

v0:
```python
import jax
import jax.numpy as jnp
from jax import lax
from jax.sharding import PartitionSpec as P

beta_one = 0.9
beta_two = 0.999
learning_rate = 0.01
correction_one = 1.0 - 0.9**20
correction_two = 1.0 - 0.999**20


def nearest_even(scaled):
    lifted = jnp.floor(scaled + 0.5)
    halfway = lifted - scaled == 0.5
    parity = lifted - 2.0 * jnp.floor(lifted * 0.5)
    return jnp.where(halfway & (parity == 1.0), lifted - 1.0, lifted)


def encode(values, scales, lowest, highest):
    return jnp.clip(nearest_even(values / scales), lowest, highest)


def cross_nodes(second_terms):
    summed = lax.psum_scatter(
        second_terms.astype(jnp.float32).astype(jnp.bfloat16),
        "node",
        scatter_dimension=0,
        tiled=True,
    ).astype(jnp.float32)
    return summed[0]


def shards(grads, first_scales, second_scales, param, first_moment, second_moment):
    locals_count = lax.axis_size("local")
    nodes_count = lax.axis_size("node")
    owned_blocks = param.shape[2]
    block_size = param.shape[3]
    values = grads.astype(jnp.float32).reshape(locals_count, nodes_count, owned_blocks, block_size)
    scale_one = first_scales.astype(jnp.float32).reshape(locals_count, nodes_count, owned_blocks, 1)
    sent_terms = (encode(values, scale_one, -8.0, 7.0) * scale_one).astype(jnp.bfloat16)
    scale_two = second_scales.astype(jnp.float32).reshape(nodes_count, owned_blocks, 1)
    partial_value = jnp.sum(
        lax.all_to_all(sent_terms, "local", split_axis=0, concat_axis=0, tiled=True).astype(
            jnp.float32
        ),
        axis=0,
    )
    second_terms = (encode(partial_value, scale_two, -127.0, 127.0) * scale_two).astype(
        jnp.bfloat16
    )
    grad_rows = cross_nodes(second_terms)
    grad_sum = grad_rows.reshape(1, 1, owned_blocks, block_size)
    new_first = beta_one * first_moment + (1.0 - beta_one) * grad_sum
    new_second = beta_two * second_moment + (1.0 - beta_two) * grad_sum * grad_sum
    new_param = param - learning_rate * (new_first / correction_one) / (
        jnp.sqrt(new_second / correction_two) + 1e-08
    )
    return (grad_sum, new_param, new_first, new_second)


def solution(mesh):
    placed = (
        P("node", "local", None, None, None),
        P("node", "local", None),
        P("node", "local"),
        P("local", "node", None, None),
        P("local", "node", None, None),
        P("local", "node", None, None),
    )
    return jax.shard_map(
        shards,
        mesh=mesh,
        in_specs=placed,
        out_specs=(
            P("local", "node", None, None),
            P("local", "node", None, None),
            P("local", "node", None, None),
            P("local", "node", None, None),
        ),
        check_vma=False,
    )
```

profile of v0, /device:TPU:8, one launch (start us, length us, event | category | flops | bytes accessed | tf_op | source)
XLA Modules:
  0.0 151.3 jit_solution(16329235548234454832)
XLA Ops:
  7.2 0.0 copy-start.3
  7.2 9.0 %reshape.57 = f32[8,4,464,128]{3,2,1,0:T(8,128)} reshape(bf16[1,1,2,64,14848]{4,3,2,1,0:T(8,128)(2,1)} %param.6) | data formatting | bytes 11403264 | tf_op jit(solution)/shard_map/reshape | solution.py:39
  16.2 0.0 copy-done.3
  16.2 0.2 convert_reduce_fusion.1
  16.3 0.1 reshape.58
  16.5 0.0 copy-start.4
  16.5 7.9 %fusion.2 = bf16[8,4,464,128]{3,2,1,0:T(8,128)(2,1)} fusion(f32[8,4,464,128]{3,2,1,0:T(8,128)} %reshape.57, f32[8,4,464]{2,1,0:T(4,128)S(1)} %reshape.58), kind=kLoop, calls=%fused_computation.3 | loop fusion | flops 30408704 | bytes 11462656 | tf_op jit(solution)/shard_map/convert_element_type | solution.py:41
  24.4 0.0 copy-start
  24.4 0.0 copy-start.1
  24.4 0.0 copy-start.2
  24.4 5.5 %all-to-all-start = ((bf16[8,4,464,128]{3,2,1,0:T(8,128)(2,1)}), bf16[8,4,464,128]{3,2,1,0:T(8,128)(2,1)}, u32[]{:S(2)}, u32[]{:S(2)}) async-start(bf16[8,4,464,128]{3,2,1,0:T(8,128)(2,1)} %fusion.2), calls=%async_computation | async-start | bytes 7602176 | tf_op jit(solution)/shard_map/all_to_all | solution.py:44
  29.8 0.0 reduce-scatter.4.cloned.1.call-start
  29.8 0.0 copy-done.4
  29.9 0.1 reshape.59
  30.0 82.0 %all-to-all-done = bf16[8,4,464,128]{3,2,1,0:T(8,128)(2,1)} async-done(((bf16[8,4,464,128]{3,2,1,0:T(8,128)(2,1)}), bf16[8,4,464,128]{3,2,1,0:T(8,128)(2,1)}, u32[]{:S(2)}, u32[]{:S(2)}) %all-to-all-start) | async-done | bytes 3801120 | tf_op jit(solution)/shard_map/all_to_all | solution.py:44
  112.0 2.7 %convert_reduce_fusion = f32[4,464,128]{2,1,0:T(8,128)S(1)} fusion(bf16[8,4,464,128]{3,2,1,0:T(8,128)(2,1)} %all-to-all-done), kind=kLoop, calls=%fused_computation.4 | loop fusion | flops 3563520 | bytes 4751360 | tf_op jit(solution)/shard_map/reduce_sum | solution.py:43
  114.7 1.4 fusion.6
  116.1 0.0 reduce-scatter.4.cloned.1.call-update
  116.1 26.4 %reduce-scatter.4.cloned.1.call-done = bf16[1,464,128]{2,1,0:T(8,128)(2,1)} async-done(((bf16[4,464,128]{2,1,0:T(8,128)(2,1)}), bf16[1,464,128]{2,1,0:T(8,128)(2,1)}) %reduce-scatter.4.cloned.1.call-update) | async-done | bytes 118800
  142.5 0.0 copy-done
  142.5 0.0 copy-done.1
  142.5 0.0 copy-done.2
  142.5 1.9 %divide_subtract_fusion = (f32[1,1,464,128]{3,2,1,0:T(8,128)}, f32[1,1,464,128]{3,2,1,0:T(8,128)}, f32[1,1,464,128]{3,2,1,0:T(8,128)}, f32[1,1,464,128]{3,2,1,0:T(8,128)}) fusion(f32[1,1,464,128]{3,2,1,0:T(8,128)S(1)} %copy-done, f32[1,1,464,128]{3,2,1,0:T(8,128)S(1)} %copy-done.1, f32[1,1,464,128]{3,2,1,0:T(8,128)S(1)} %copy-done.2, ...), kind=kLoop, calls=%fused_computation.19 | loop fusion | flops 772096 | bytes 1781760 | tf_op jit(solution)/shard_map/sub | solution.py:56
  (1 shorter events, 0.0 us)
Async XLA Ops:
  7.2 9.0 %copy-start.3 = (bf16[1,1,14848]{2,1,0:T(2,128)(2,1)S(1)}, bf16[1,1,14848]{2,1,0:T(2,128)(2,1)}, u32[]{:S(2)}) copy-start(bf16[1,1,14848]{2,1,0:T(2,128)(2,1)} %param.7) | copy-start | bytes 89092
  16.5 13.4 %copy-start.4 = (bf16[1,1856]{1,0:T(2,128)(2,1)S(1)}, bf16[1,1856]{1,0:T(2,128)(2,1)}, u32[]{:S(2)}) copy-start(bf16[1,1856]{1,0:T(2,128)(2,1)} %param.8) | copy-start | bytes 11140
  24.4 118.2 %copy-start = (f32[1,1,464,128]{3,2,1,0:T(8,128)S(1)}, f32[1,1,464,128]{3,2,1,0:T(8,128)}, u32[]{:S(2)}) copy-start(f32[1,1,464,128]{3,2,1,0:T(8,128)} %param.9) | copy-start | bytes 712708
  24.4 118.2 %copy-start.1 = (f32[1,1,464,128]{3,2,1,0:T(8,128)S(1)}, f32[1,1,464,128]{3,2,1,0:T(8,128)}, u32[]{:S(2)}) copy-start(f32[1,1,464,128]{3,2,1,0:T(8,128)} %param.10) | copy-start | bytes 712708
  24.4 118.2 %copy-start.2 = (f32[1,1,464,128]{3,2,1,0:T(8,128)S(1)}, f32[1,1,464,128]{3,2,1,0:T(8,128)}, u32[]{:S(2)}) copy-start(f32[1,1,464,128]{3,2,1,0:T(8,128)} %param.11) | copy-start | bytes 712708
  24.4 87.6 %all-to-all-start = ((bf16[8,4,464,128]{3,2,1,0:T(8,128)(2,1)}), bf16[8,4,464,128]{3,2,1,0:T(8,128)(2,1)}, u32[]{:S(2)}, u32[]{:S(2)}) async-start(bf16[8,4,464,128]{3,2,1,0:T(8,128)(2,1)} %fusion.2), calls=%async_computation | async-start | bytes 7602176 | tf_op jit(solution)/shard_map/all_to_all | solution.py:44
  29.8 112.7 %reduce-scatter.4.cloned.1.call-start = ((), (), s32[]{:S(2)}) async-start(), calls=%async_computation.2 | async-start | bytes 593920
Sparse Core Ops, SparseCore 0:
  116.2 26.2 reduce-scatter.3
where the time goes:
time: 153 us; the launch traced here: 151 us
  waiting for transfers between devices  108 us (71%)
  other arithmetic  14.1 us (9%)
  between operations  14.1 us (9%)
  local copies, waits for them, and re-layouts  9.22 us (6%)
  starting transfers between devices  5.46 us (4%)
    all_to_all x1, waiting for transfers between devices, shards(): lax.all_to_all(sent_terms, 'local', split_axis=0, concat_axis=0, tiled=True)  82 us
    unnamed x2, waiting for transfers between devices  26.5 us
    reshape x1, local copies, waits for them, and re-layouts, shards(): grads.astype(jnp.float32)  9 us
    convert_element_type x1, other arithmetic, shards(): (encode(values, scale_one, -8.0, 7.0) * scale_one).astype(jnp.bfloat16)  7.91 us
    all_to_all x1, starting transfers between devices, shards(): lax.all_to_all(sent_terms, 'local', split_axis=0, concat_axis=0, tiled=True)  5.46 us
  transfers between devices with their start and end apart: 2, of which 2 were waited for; matrix products, arithmetic and copies ran while one was open for 0% of the time, Pallas kernels for 0%

commit v1 on v0

v1 whole, which is shorter than its diff:
```python
import functools

import jax
import jax.numpy as jnp
from jax import lax
from jax.experimental import pallas as pl
from jax.experimental.pallas import tpu as pltpu
from jax.sharding import PartitionSpec as P

beta_one = 0.9
beta_two = 0.999
learning_rate = 0.01
correction_one = 1.0 - 0.9**20
correction_two = 1.0 - 0.999**20

LANES = 128
TILE_ROWS = 16
ROUNDER = 1.5 * 2.0**23


def nearest_even(scaled):
    lifted = jnp.floor(scaled + 0.5)
    halfway = lifted - scaled == 0.5
    parity = lifted - 2.0 * jnp.floor(lifted * 0.5)
    return jnp.where(halfway & (parity == 1.0), lifted - 1.0, lifted)


def encode(values, scales, lowest, highest):
    return jnp.clip(nearest_even(values / scales), lowest, highest)


def adam(grad_sum, param, first_moment, second_moment):
    new_first = beta_one * first_moment + (1.0 - beta_one) * grad_sum
    new_second = beta_two * second_moment + (1.0 - beta_two) * grad_sum * grad_sum
    new_param = param - learning_rate * (new_first / correction_one) / (
        jnp.sqrt(new_second / correction_two) + 1e-08
    )
    return new_param, new_first, new_second


def plain_sum(grads, first_scales, second_scales, owned_blocks, block_size):
    locals_count = lax.axis_size("local")
    nodes_count = lax.axis_size("node")
    values = grads.astype(jnp.float32).reshape(locals_count, nodes_count, owned_blocks, block_size)
    scale_one = first_scales.astype(jnp.float32).reshape(locals_count, nodes_count, owned_blocks, 1)
    sent_terms = (encode(values, scale_one, -8.0, 7.0) * scale_one).astype(jnp.bfloat16)
    scale_two = second_scales.astype(jnp.float32).reshape(nodes_count, owned_blocks, 1)
    partial_value = jnp.sum(
        lax.all_to_all(sent_terms, "local", split_axis=0, concat_axis=0, tiled=True).astype(
            jnp.float32
        ),
        axis=0,
    )
    second_terms = (encode(partial_value, scale_two, -127.0, 127.0) * scale_two).astype(
        jnp.bfloat16
    )
    summed = lax.psum_scatter(second_terms, "node", scatter_dimension=0, tiled=True)
    return summed[0].astype(jnp.float32)


def round_to(values, scale, lowest, highest):
    big = scale * ROUNDER
    return jnp.clip((values + big) - big, scale * lowest, scale * highest)


def pieces_of(columns):
    fours = columns // 4
    count = min(PIECES, fours)
    sizes = [4 * (fours // count + (1 if i < fours % count else 0)) for i in range(count)]
    starts = [sum(sizes[:i]) for i in range(count)]
    return list(zip(starts, sizes))


PIECES = 4


def reduce_kernel(
    pieces,
    grads_ref,
    scale_one_ref,
    scale_two_ref,
    out_ref,
    loaded,
    cross_out,
    cross_in,
    sums,
    joined_in,
    near_in,
    far_in,
    node_out,
    node_in,
    load_sem,
    cross_send,
    cross_recv,
    half_send,
    joined_recv,
    near_recv,
    far_send,
    far_recv,
    node_send,
    node_recv,
):
    node = lax.axis_index("node")
    local = lax.axis_index("local")
    z, core = local // 2, local % 2
    half = z // 2
    inner = (z + half) % 2 == 1
    partner = z + 1 - 2 * (z % 2)
    other_inner, other_outer = 2 - half, 3 - 3 * half
    nodes = lax.axis_size("node")
    columns_of = scale_two_ref.shape[-1]
    count = len(pieces)

    def at(z_to, core_to, node_to=None):
        return (node if node_to is None else node_to, 2 * z_to + core_to)

    def destination(order):
        return jnp.where(
            order == 0,
            other_outer,
            jnp.where(order == 1, other_inner, jnp.where(order == 2, partner, z)),
        )

    def lanes(p):
        start, size = pieces[p]
        return pl.ds(start * LANES, size * LANES)

    def quarter(p):
        start, size = pieces[p]
        return pl.ds(start // 4 * LANES, size // 4 * LANES)

    barrier = pltpu.get_barrier_semaphore()
    peers = [at(z, 1 - core)]
    peers += [at((z + k) % 4, core) for k in range(1, 4)]
    peers += [(lax.rem(node + k, nodes), local) for k in range(1, 4)]
    for peer in peers:
        pl.semaphore_signal(barrier, inc=1, device_id=peer, device_id_type=pl.DeviceIdType.MESH)

    def load(order, p):
        z_to = destination(order)
        return pltpu.make_async_copy(
            grads_ref.at[pl.ds(2 * z_to, 2), :, lanes(p)],
            loaded.at[order, :, :, lanes(p)],
            load_sem.at[order, p],
        )

    for order in range(4):
        for p in range(count):
            load(order, p).start()

    def cross(order, p):
        return pltpu.make_async_remote_copy(
            src_ref=cross_out.at[order, :, lanes(p)],
            dst_ref=cross_in.at[order, :, lanes(p)],
            send_sem=cross_send.at[order, p],
            recv_sem=cross_recv.at[order, p],
            device_id=at(z, 1 - core),
            device_id_type=pl.DeviceIdType.MESH,
        )

    def to_join(order, p):
        return pltpu.make_async_remote_copy(
            src_ref=sums.at[order, :, lanes(p)],
            dst_ref=joined_in.at[order, :, lanes(p)],
            send_sem=half_send.at[order, p],
            recv_sem=joined_recv.at[order, p],
            device_id=at(partner, core),
            device_id_type=pl.DeviceIdType.MESH,
        )

    def to_near(p):
        return pltpu.make_async_remote_copy(
            src_ref=sums.at[2, :, lanes(p)],
            dst_ref=near_in.at[:, lanes(p)],
            send_sem=half_send.at[2, p],
            recv_sem=near_recv.at[p],
            device_id=at(partner, core),
            device_id_type=pl.DeviceIdType.MESH,
        )

    def to_far(order, p):
        return pltpu.make_async_remote_copy(
            src_ref=sums.at[order, :, lanes(p)],
            dst_ref=far_in.at[:, lanes(p)],
            send_sem=far_send.at[order, p],
            recv_sem=far_recv.at[p],
            device_id=at(destination(order), core),
            device_id_type=pl.DeviceIdType.MESH,
        )

    def to_node(k, p):
        other = lax.rem(node + k, nodes)
        return pltpu.make_async_remote_copy(
            src_ref=node_out.at[other, :, quarter(p)],
            dst_ref=node_in.at[k - 1, :, quarter(p)],
            send_sem=node_send.at[k - 1, p],
            recv_sem=node_recv.at[k - 1, p],
            device_id=(other, local),
            device_id_type=pl.DeviceIdType.MESH,
        )

    def code(order, p, core_to, target):
        chunk = 2 * destination(order) + core_to
        start, size = pieces[p]
        scales = scale_one_ref[chunk]
        for j in range(start, start + size):
            cols = slice(j * LANES, (j + 1) * LANES)
            scale = jnp.broadcast_to(scales[:, j : j + 1], (TILE_ROWS, LANES))
            values = loaded[order, core_to, :, cols].astype(jnp.float32)
            target[order, :, cols] = round_to(values, scale, -8.0, 7.0).astype(jnp.bfloat16)

    def pair_sum(order, p):
        cross(order, p).wait_recv()
        start, size = pieces[p]
        sums[order, :, lanes(p)] = (
            sums[order, :, lanes(p)].astype(jnp.float32)
            + cross_in[order, :, lanes(p)].astype(jnp.float32)
        ).astype(jnp.bfloat16)

        @pl.when(jnp.logical_and(order < 2, jnp.logical_not(inner)))
        def _():
            to_join(order, p).start()

        @pl.when(order == 2)
        def _():
            to_near(p).start()

    def first_phase(order, carry):
        for p in range(count):
            load(order, p).wait()
            code(order, p, 1 - core, cross_out)
            if p == 0:

                @pl.when(order == 0)
                def _():
                    pl.semaphore_wait(barrier, len(peers))

            cross(order, p).start()
            code(order, p, core, sums)
            if p > 0:
                pair_sum(order, p - 1)
            else:

                @pl.when(order > 0)
                def _():
                    pair_sum(order - 1, count - 1)

        return carry

    lax.fori_loop(0, 4, first_phase, 0)
    pair_sum(3, count - 1)

    @pl.when(inner)
    def _():
        for order in range(2):
            for p in range(count):
                to_join(order, p).wait_recv()
                sums[order, :, lanes(p)] = (
                    sums[order, :, lanes(p)].astype(jnp.float32)
                    + joined_in[order, :, lanes(p)].astype(jnp.float32)
                ).astype(jnp.bfloat16)
                to_far(order, p).start()

    scales_two = scale_two_ref[...]

    def recode(p):
        to_far(0, p).wait_recv()
        to_near(p).wait_recv()
        start, size = pieces[p]
        step = size // 4
        for k in range(step):
            terms = []
            for q in range(4):
                j = start + q * step + k
                cols = slice(j * LANES, (j + 1) * LANES)
                scale = jnp.broadcast_to(scales_two[:, j : j + 1], (TILE_ROWS, LANES))
                total = (
                    sums[3, :, cols].astype(jnp.float32)
                    + near_in[:, cols].astype(jnp.float32)
                    + far_in[:, cols].astype(jnp.float32)
                )
                terms.append(round_to(total, scale, -127.0, 127.0))
            where = slice((start // 4 + k) * LANES, (start // 4 + k + 1) * LANES)
            for n in range(4):
                node_out[n, :, where] = jnp.concatenate(
                    [term[4 * n : 4 * n + 4] for term in terms], axis=0
                ).astype(jnp.bfloat16)
        for k in range(1, 4):
            to_node(k, p).start()

    def collect(p):
        for k in range(1, 4):
            to_node(k, p).wait_recv()
        start, size = pieces[p]
        step = size // 4
        for k in range(step):
            where = slice((start // 4 + k) * LANES, (start // 4 + k + 1) * LANES)
            total = node_out[node, :, where].astype(jnp.float32)
            for i in range(3):
                total = total + node_in[i, :, where].astype(jnp.float32)
            for q in range(4):
                j = start + q * step + k
                out_ref[pl.ds(j, 4, stride=columns_of), :] = total[4 * q : 4 * q + 4]

    for p in range(count):
        recode(p)
        if p > 0:
            collect(p - 1)
    collect(count - 1)

    for p in range(count):
        for order in range(4):
            cross(order, p).wait_send()
        to_near(p).wait_send()
        for k in range(1, 4):
            to_node(k, p).wait_send()

    @pl.when(inner)
    def _():
        for p in range(count):
            for order in range(2):
                to_far(order, p).wait_send()

    @pl.when(jnp.logical_not(inner))
    def _():
        for p in range(count):
            for order in range(2):
                to_join(order, p).wait_send()


def line_sum(grads, first_scales, second_scales, owned_blocks, block_size):
    locals_count = lax.axis_size("local")
    depth = grads.shape[-1]
    columns = depth // block_size
    pieces = pieces_of(columns)
    count = len(pieces)
    rows = TILE_ROWS
    scratch = [
        pltpu.VMEM((4, 2, rows, depth), jnp.bfloat16),
        pltpu.VMEM((4, rows, depth), jnp.bfloat16),
        pltpu.VMEM((4, rows, depth), jnp.bfloat16),
        pltpu.VMEM((4, rows, depth), jnp.bfloat16),
        pltpu.VMEM((2, rows, depth), jnp.bfloat16),
        pltpu.VMEM((rows, depth), jnp.bfloat16),
        pltpu.VMEM((rows, depth), jnp.bfloat16),
        pltpu.VMEM((4, rows, depth // 4), jnp.bfloat16),
        pltpu.VMEM((3, rows, depth // 4), jnp.bfloat16),
    ]
    sems = [(4, count)] * 3
    sems += [(3, count), (2, count), (count,), (2, count), (count,), (3, count), (3, count)]
    return pl.pallas_call(
        functools.partial(reduce_kernel, pieces),
        out_shape=jax.ShapeDtypeStruct((owned_blocks, block_size), jnp.float32),
        in_specs=[
            pl.BlockSpec(memory_space=pl.ANY),
            pl.BlockSpec(memory_space=pltpu.VMEM),
            pl.BlockSpec(memory_space=pltpu.VMEM),
        ],
        out_specs=pl.BlockSpec(memory_space=pltpu.VMEM),
        scratch_shapes=scratch + [pltpu.SemaphoreType.DMA(shape) for shape in sems],
        compiler_params=pltpu.CompilerParams(
            collective_id=0, has_side_effects=True, vmem_limit_bytes=40 * 2**20
        ),
    )(
        grads.reshape(locals_count, rows, depth),
        first_scales.astype(jnp.float32).reshape(locals_count, rows, columns),
        second_scales.astype(jnp.float32).reshape(rows, columns),
    )


def shards(grads, first_scales, second_scales, param, first_moment, second_moment):
    owned_blocks, block_size = param.shape[2:]
    nodes_count, locals_count = lax.axis_size("node"), lax.axis_size("local")
    depth = grads.shape[-1]
    columns = depth // block_size
    fits = (
        nodes_count == 4
        and locals_count == 8
        and block_size == LANES
        and depth % block_size == 0
        and columns % 4 == 0
        and owned_blocks == 4 * columns
        and grads.shape[-2] % TILE_ROWS == 0
    )
    reduced = line_sum if fits else plain_sum
    grad_sum = reduced(grads, first_scales, second_scales, owned_blocks, block_size)
    grad_sum = grad_sum.reshape(1, 1, owned_blocks, block_size)
    return (grad_sum, *adam(grad_sum, param, first_moment, second_moment))


def solution(mesh):
    owned = P("local", "node", None, None)
    return jax.shard_map(
        shards,
        mesh=mesh,
        in_specs=(
            P("node", "local", None, None, None),
            P("node", "local", None),
            P("node", "local"),
            owned,
            owned,
            owned,
        ),
        out_specs=(owned,) * 4,
        check_vma=False,
    )
```

time: 153 us -> 48.8 us (0.32); the launches traced: 151 us -> 48.6 us
  waiting for transfers between devices: 108 us -> 0 us
  Pallas kernels: 0 us -> 42.2 us
  between operations: 14.1 us -> 0.7 us
  other arithmetic: 14.1 us -> 2.69 us
  local copies, waits for them, and re-layouts: 9.22 us -> 3 us
  starting transfers between devices: 5.46 us -> 0 us
    all_to_all x1 -> x0, waiting for transfers between devices: 82 us -> none  [shards(): lax.all_to_all(sent_terms, 'local', split_axis=0, concat_axis=0, tiled=True)]
    pallas_call x0 -> x1, Pallas kernels: none -> 42.2 us  [line_sum(): pl.pallas_call(functools.partial(reduce_kernel, pieces), out_shape=jax.Sh...]
    unnamed x2 -> x0, waiting for transfers between devices: 26.5 us -> none
    convert_element_type x2 -> x0, other arithmetic: 9.28 us -> none  [the longest x1 7.91 us: shards(): (encode(values, scale_one, -8.0, 7.0) * scale_one).astype(jnp.bfloat16)]
    reshape x1 -> x2, local copies, waits for them, and re-layouts: 9 us -> 0.22 us  [the longest x1 0.14 us: line_sum(): first_scales.astype(jnp.float32).reshape(locals_count, rows, columns)]
    all_to_all x1 -> x0, starting transfers between devices: 5.46 us -> none  [shards(): lax.all_to_all(sent_terms, 'local', split_axis=0, concat_axis=0, tiled=True)]
    unnamed x10 -> x9, local copies, waits for them, and re-layouts: 0.02 us -> 2.77 us
    reduce_sum x1 -> x0, other arithmetic: 2.72 us -> none  [shards(): jnp.sum(lax.all_to_all(sent_terms, 'local', split_axis=0, concat_axis=0,...]
  transfers between devices with their start and end apart: 2 -> 0, of which waited for: 2 -> 0; matrix products, arithmetic and copies ran while one was open for 0% -> 0% of each run, Pallas kernels for 0% -> 0%
where the time goes in v1:
time: 48.8 us; the launch traced here: 48.6 us
  Pallas kernels  42.2 us (86%)
  local copies, waits for them, and re-layouts  3 us (6%)
  other arithmetic  2.69 us (6%)
  between operations  0.7 us (1%)
    pallas_call x1, Pallas kernels, line_sum(): pl.pallas_call(functools.partial(reduce_kernel, pieces), out_shape=jax.Sh...  42.2 us
    unnamed x9, local copies, waits for them, and re-layouts  2.77 us
    reshape x1, other arithmetic, line_sum(): first_scales.astype(jnp.float32).reshape(locals_count, rows, columns)  0.99 us

profile of v1, /device:TPU:8, one launch (start us, length us, event | category | flops | bytes accessed | tf_op | source)
XLA Modules:
  0.0 48.6 jit_solution(9465406010747260934)
XLA Ops:
  0.6 0.0 copy-start.1
  0.6 0.8 %convert_reduce_fusion.1 = f32[1856]{0:T(1024)S(1)} fusion(bf16[1,1856]{1,0:T(2,128)(2,1)} %param.8), kind=kLoop, calls=%fused_computation.6 | loop fusion | flops 1856 | bytes 11136 | tf_op jit(solution)/shard_map/reshape | solution.py:367
  1.4 0.1 reshape.36.scale_two_ref
  1.5 1.0 %convert_reduce_fusion = f32[14848]{0:T(1024)S(1)} fusion(bf16[1,1,14848]{2,1,0:T(2,128)(2,1)} %param.7), kind=kLoop, calls=%fused_computation.5 | loop fusion | flops 14848 | bytes 89088 | tf_op jit(solution)/shard_map/reshape | solution.py:366
  2.5 0.1 reshape.34.scale_one_ref
  2.6 0.0 copy-start
  2.6 2.1 %copy-done = bf16[1,1,2,64,14848]{4,3,2,1,0:T(8,128)(2,1)S(1)} copy-done((bf16[1,1,2,64,14848]{4,3,2,1,0:T(8,128)(2,1)S(1)}, bf16[1,1,2,64,14848]{4,3,2,1,0:T(8,128)(2,1)}, u32[]{:S(2)}) %copy-start) | copy-done | bytes 3801112
  4.7 0.0 copy-start.2
  4.7 0.0 copy-start.3
  4.7 42.2 %shard_map.93 = f32[464,128]{1,0:T(8,128)S(1)} custom-call(bf16[8,16,14848]{2,1,0:T(8,128)(2,1)S(1)} %bitcast.10, f32[8,16,116]{2,1,0:T(8,128)S(1)} %reshape.34.scale_one_ref, f32[16,116]{1,0:T(8,128)S(1)} %reshape.36.scale_two_ref), custom_call_target="tpu_custom_call" | custom-call | tf_op jit(solution)/shard_map/pallas_call | solution.py:351
  47.0 0.0 copy-done.1
  47.0 0.0 copy-done.2
  47.0 0.0 copy-done.3
  47.0 0.9 %divide_subtract_fusion = (f32[1,1,464,128]{3,2,1,0:T(8,128)}, f32[1,1,464,128]{3,2,1,0:T(8,128)}, f32[1,1,464,128]{3,2,1,0:T(8,128)}) fusion(f32[1,1,464,128]{3,2,1,0:T(8,128)S(1)} %copy-done.1, f32[464,128]{1,0:T(8,128)S(1)} %shard_map.93, f32[1,1,464,128]{3,2,1,0:T(8,128)S(1)} %copy-done.2, f32[1,1,464,128]{3,2,1,0:T(8,128)S(1)} %copy-done.3), kind=kLoop, calls=%fused_computation.4 | loop fusion | flops 712704 | bytes 1662976 | tf_op jit(solution)/shard_map/sub | solution.py:35
  47.9 0.7 %copy.11 = f32[1,1,464,128]{3,2,1,0:T(8,128)} copy(f32[1,1,464,128]{3,2,1,0:T(8,128)S(1)} %bitcast.11) | data formatting | bytes 475136
Async XLA Ops:
  0.6 46.3 %copy-start.1 = (f32[1,1,464,128]{3,2,1,0:T(8,128)S(1)}, f32[1,1,464,128]{3,2,1,0:T(8,128)}, u32[]{:S(2)}) copy-start(f32[1,1,464,128]{3,2,1,0:T(8,128)} %param.9) | copy-start | bytes 712708
  2.6 2.1 %copy-start = (bf16[1,1,2,64,14848]{4,3,2,1,0:T(8,128)(2,1)S(1)}, bf16[1,1,2,64,14848]{4,3,2,1,0:T(8,128)(2,1)}, u32[]{:S(2)}) copy-start(bf16[1,1,2,64,14848]{4,3,2,1,0:T(8,128)(2,1)} %param.6) | copy-start | bytes 11403268
  4.7 42.3 %copy-start.2 = (f32[1,1,464,128]{3,2,1,0:T(8,128)S(1)}, f32[1,1,464,128]{3,2,1,0:T(8,128)}, u32[]{:S(2)}) copy-start(f32[1,1,464,128]{3,2,1,0:T(8,128)} %param.10) | copy-start | bytes 712708
  4.7 42.3 %copy-start.3 = (f32[1,1,464,128]{3,2,1,0:T(8,128)S(1)}, f32[1,1,464,128]{3,2,1,0:T(8,128)}, u32[]{:S(2)}) copy-start(f32[1,1,464,128]{3,2,1,0:T(8,128)} %param.11) | copy-start | bytes 712708

commit v2 on v1

--- a/solution.py
+++ b/solution.py
@@ -63,24 +63,50 @@
     return jnp.clip((values + big) - big, scale * lowest, scale * highest)
 
 
+def unfold(flat, first_row, columns, target):
+    lane = lax.broadcasted_iota(jnp.int32, (1, LANES), 1)
+    width = flat.shape[-1]
+
+    def tile(a):
+        held = flat[:, a * LANES : min((a + 1) * LANES, width)].astype(jnp.float32)
+        short = LANES - held.shape[-1]
+        return jnp.concatenate([held, jnp.zeros((1, short), jnp.float32)], 1) if short else held
+
+    for r in range(TILE_ROWS):
+        a, offset = divmod((first_row + r) * columns, LANES)
+        row = tile(a)
+        if offset:
+            row = pltpu.roll(row, LANES - offset, 1)
+        if offset + columns > LANES:
+            after = pltpu.roll(tile(a + 1), LANES - offset, 1)
+            row = jnp.where(lane < LANES - offset, row, after)
+        target[r : r + 1, :] = row
+
+
 def pieces_of(columns):
     fours = columns // 4
-    count = min(PIECES, fours)
-    sizes = [4 * (fours // count + (1 if i < fours % count else 0)) for i in range(count)]
-    starts = [sum(sizes[:i]) for i in range(count)]
+    shares = SHARES if fours >= sum(SHARES) else (1,)
+    sizes = [fours * share // sum(shares) for share in shares]
+    sizes[0] += fours - sum(sizes)
+    sizes = [4 * size for size in sizes]
+    starts = [sum(sizes[:i]) for i in range(len(sizes))]
     return list(zip(starts, sizes))
 
 
-PIECES = 4
+SHARES = (11, 10, 8)
 
 
 def reduce_kernel(
     pieces,
     grads_ref,
+    flat_one_ref,
+    flat_two_ref,
+    out_ref,
+    loaded,
+    flat_one,
+    flat_two,
     scale_one_ref,
     scale_two_ref,
-    out_ref,
-    loaded,
     cross_out,
     cross_in,
     sums,
@@ -89,6 +115,7 @@
     far_in,
     node_out,
     node_in,
+    scale_sem,
     load_sem,
     cross_send,
     cross_recv,
@@ -108,7 +135,7 @@
     partner = z + 1 - 2 * (z % 2)
     other_inner, other_outer = 2 - half, 3 - 3 * half
     nodes = lax.axis_size("node")
-    columns_of = scale_two_ref.shape[-1]
+    columns_of = grads_ref.shape[-1] // LANES
     count = len(pieces)
 
     def at(z_to, core_to, node_to=None):
@@ -144,9 +171,19 @@
             load_sem.at[order, p],
         )
 
+    flat_copies = [
+        pltpu.make_async_copy(flat_one_ref, flat_one, scale_sem.at[0]),
+        pltpu.make_async_copy(flat_two_ref, flat_two, scale_sem.at[1]),
+    ]
+    flat_copies[0].start()
     for order in range(4):
         for p in range(count):
             load(order, p).start()
+    flat_copies[1].start()
+
+    flat_copies[0].wait()
+    for chunk in range(scale_one_ref.shape[0]):
+        unfold(flat_one, chunk * TILE_ROWS, columns_of, scale_one_ref.at[chunk])
 
     def cross(order, p):
         return pltpu.make_async_remote_copy(
@@ -237,18 +274,16 @@
 
             cross(order, p).start()
             code(order, p, core, sums)
-            if p > 0:
-                pair_sum(order, p - 1)
-            else:
-
-                @pl.when(order > 0)
-                def _():
-                    pair_sum(order - 1, count - 1)
+
+            @pl.when(order > 0)
+            def _(p=p):
+                pair_sum(order - 1, p)
 
         return carry
 
     lax.fori_loop(0, 4, first_phase, 0)
-    pair_sum(3, count - 1)
+    for p in range(count):
+        pair_sum(3, p)
 
     @pl.when(inner)
     def _():
@@ -261,6 +296,8 @@
                 ).astype(jnp.bfloat16)
                 to_far(order, p).start()
 
+    flat_copies[1].wait()
+    unfold(flat_two, 0, columns_of, scale_two_ref)
     scales_two = scale_two_ref[...]
 
     def recode(p):
@@ -331,12 +368,15 @@
 def line_sum(grads, first_scales, second_scales, owned_blocks, block_size):
     locals_count = lax.axis_size("local")
     depth = grads.shape[-1]
-    columns = depth // block_size
-    pieces = pieces_of(columns)
+    pieces = pieces_of(depth // block_size)
     count = len(pieces)
     rows = TILE_ROWS
     scratch = [
         pltpu.VMEM((4, 2, rows, depth), jnp.bfloat16),
+        pltpu.VMEM((1, first_scales.shape[-1]), jnp.bfloat16),
+        pltpu.VMEM((1, second_scales.shape[-1]), jnp.bfloat16),
+        pltpu.VMEM((locals_count, rows, LANES), jnp.float32),
+        pltpu.VMEM((rows, LANES), jnp.float32),
         pltpu.VMEM((4, rows, depth), jnp.bfloat16),
         pltpu.VMEM((4, rows, depth), jnp.bfloat16),
         pltpu.VMEM((4, rows, depth), jnp.bfloat16),
@@ -346,26 +386,50 @@
         pltpu.VMEM((4, rows, depth // 4), jnp.bfloat16),
         pltpu.VMEM((3, rows, depth // 4), jnp.bfloat16),
     ]
-    sems = [(4, count)] * 3
+    sems = [(2,)] + [(4, count)] * 3
     sems += [(3, count), (2, count), (count,), (2, count), (count,), (3, count), (3, count)]
     return pl.pallas_call(
         functools.partial(reduce_kernel, pieces),
         out_shape=jax.ShapeDtypeStruct((owned_blocks, block_size), jnp.float32),
         in_specs=[
             pl.BlockSpec(memory_space=pl.ANY),
-            pl.BlockSpec(memory_space=pltpu.VMEM),
-            pl.BlockSpec(memory_space=pltpu.VMEM),
+            pl.BlockSpec(memory_space=pl.ANY),
+            pl.BlockSpec(memory_space=pl.ANY),
         ],
         out_specs=pl.BlockSpec(memory_space=pltpu.VMEM),
         scratch_shapes=scratch + [pltpu.SemaphoreType.DMA(shape) for shape in sems],
         compiler_params=pltpu.CompilerParams(
-            collective_id=0, has_side_effects=True, vmem_limit_bytes=40 * 2**20
+            collective_id=0, has_side_effects=True, vmem_limit_bytes=61 * 2**20
         ),
     )(
         grads.reshape(locals_count, rows, depth),
-        first_scales.astype(jnp.float32).reshape(locals_count, rows, columns),
-        second_scales.astype(jnp.float32).reshape(rows, columns),
-    )
+        first_scales.reshape(1, -1),
+        second_scales,
+    )
+
+
+def adam_kernel(reduced, param, first, second, grad_sum, new_param, new_first, new_second):
+    total = reduced[...]
+    grad_sum[...] = total
+    new_param[...], new_first[...], new_second[...] = adam(
+        total, param[...], first[...], second[...]
+    )
+
+
+def finish(reduced, param, first_moment, second_moment):
+    shape = reduced.shape
+    steps = 2 if shape[0] % 16 == 0 else 1
+    block = pl.BlockSpec((shape[0] // steps, shape[1]), lambda i: (i, 0))
+    return pl.pallas_call(
+        adam_kernel,
+        out_shape=[jax.ShapeDtypeStruct(shape, jnp.float32)] * 4,
+        grid=(steps,),
+        in_specs=[block] * 4,
+        out_specs=[block] * 4,
+        cost_estimate=pl.CostEstimate(
+            flops=16 * reduced.size, bytes_accessed=32 * reduced.size, transcendentals=reduced.size
+        ),
+    )(reduced, param.reshape(shape), first_moment.reshape(shape), second_moment.reshape(shape))
 
 
 def shards(grads, first_scales, second_scales, param, first_moment, second_moment):
@@ -382,9 +446,12 @@
         and owned_blocks == 4 * columns
         and grads.shape[-2] % TILE_ROWS == 0
     )
-    reduced = line_sum if fits else plain_sum
-    grad_sum = reduced(grads, first_scales, second_scales, owned_blocks, block_size)
-    grad_sum = grad_sum.reshape(1, 1, owned_blocks, block_size)
+    if fits:
+        reduced = line_sum(grads, first_scales, second_scales, owned_blocks, block_size)
+        outputs = finish(reduced, param, first_moment, second_moment)
+        return tuple(output.reshape(param.shape) for output in outputs)
+    grad_sum = plain_sum(grads, first_scales, second_scales, owned_blocks, block_size)
+    grad_sum = grad_sum.reshape(param.shape)
     return (grad_sum, *adam(grad_sum, param, first_moment, second_moment))
 
 

time: 48.8 us -> 45.9 us (0.941)
  local copies, waits for them, and re-layouts: 3 us -> 0 us
  Pallas kernels: 42.2 us -> 45.1 us
  other arithmetic: 2.69 us -> 0 us
    unnamed x9 -> x0, local copies, waits for them, and re-layouts: 2.77 us -> none
    pallas_call x0 -> x1, Pallas kernels: none -> 2.1 us  [finish(): pl.pallas_call(adam_kernel, out_shape=[jax.ShapeDtypeStruct(shape, jnp.fl...]
    reshape x2 -> x0, other arithmetic: 1.75 us -> none  [the longest x1 0.99 us: line_sum(): first_scales.astype(jnp.float32).reshape(locals_count, rows, columns)]
    sub x1 -> x0, other arithmetic: 0.94 us -> none  [adam(): param - learning_rate * (new_first / correction_one) / (jnp.sqrt(new_seco...]
    pallas_call x1, Pallas kernels: 42.2 us -> 43 us  [line_sum(): pl.pallas_call(functools.partial(reduce_kernel, pieces), out_shape=jax.Sh...]
where the time goes in v2:
time: 45.9 us; the launch traced here: 45.7 us
  Pallas kernels  45.1 us (98%)
  between operations  0.64 us (1%)
    pallas_call x1, Pallas kernels, line_sum(): pl.pallas_call(functools.partial(reduce_kernel, pieces), out_shape=jax.Sh...  43 us
    pallas_call x1, Pallas kernels, finish(): pl.pallas_call(adam_kernel, out_shape=[jax.ShapeDtypeStruct(shape, jnp.fl...  2.1 us

profile of v2, /device:TPU:8, one launch (start us, length us, event | category | flops | bytes accessed | tf_op | source)
XLA Modules:
  0.0 45.7 jit_solution(12041284219453779719)
XLA Ops:
  0.6 43.0 %shard_map.93.reduced = f32[464,128]{1,0:T(8,128)} custom-call(bf16[8,16,14848]{2,1,0:T(8,128)(2,1)} %bitcast.9, bf16[1,14848]{1,0:T(2,128)(2,1)} %bitcast.13, bf16[1,1856]{1,0:T(2,128)(2,1)} %flat_two_ref.1), custom_call_target="tpu_custom_call" | custom-call | tf_op jit(solution)/shard_map/pallas_call | solution.py:391
  43.6 2.1 %shard_map.94 = (f32[464,128]{1,0:T(8,128)}, f32[464,128]{1,0:T(8,128)}, f32[464,128]{1,0:T(8,128)}, f32[464,128]{1,0:T(8,128)}) custom-call(f32[464,128]{1,0:T(8,128)} %shard_map.93.reduced, f32[464,128]{1,0:T(8,128)} %bitcast.10, f32[464,128]{1,0:T(8,128)} %bitcast.11, f32[464,128]{1,0:T(8,128)} %bitcast.12), custom_call_target="tpu_custom_call" | custom-call | flops 950272 | bytes 1900544 | tf_op jit(solution)/shard_map/pallas_call | solution.py:423

commit v3 on v2

--- a/solution.py
+++ b/solution.py
@@ -182,8 +182,6 @@
     flat_copies[1].start()
 
     flat_copies[0].wait()
-    for chunk in range(scale_one_ref.shape[0]):
-        unfold(flat_one, chunk * TILE_ROWS, columns_of, scale_one_ref.at[chunk])
 
     def cross(order, p):
         return pltpu.make_async_remote_copy(
@@ -263,6 +261,13 @@
             to_near(p).start()
 
     def first_phase(order, carry):
+        for z_to in range(scale_one_ref.shape[0] // 2):
+
+            @pl.when(destination(order) == z_to)
+            def _(z_to=z_to):
+                for chunk in (2 * z_to, 2 * z_to + 1):
+                    unfold(flat_one, chunk * TILE_ROWS, columns_of, scale_one_ref.at[chunk])
+
         for p in range(count):
             load(order, p).wait()
             code(order, p, 1 - core, cross_out)

time: 45.9 us -> 45.9 us (level)
  no operation moved by 1% of the time
where the time goes in v3:
time: 45.9 us; the launch traced here: 45.7 us
  Pallas kernels  45.1 us (98%)
  between operations  0.64 us (1%)
    pallas_call x1, Pallas kernels, line_sum(): pl.pallas_call(functools.partial(reduce_kernel, pieces), out_shape=jax.Sh...  43 us
    pallas_call x1, Pallas kernels, finish(): pl.pallas_call(adam_kernel, out_shape=[jax.ShapeDtypeStruct(shape, jnp.fl...  2.1 us

profile of v3, /device:TPU:8, one launch (start us, length us, event | category | flops | bytes accessed | tf_op | source)
XLA Modules:
  0.0 45.7 jit_solution(1273469110531696151)
XLA Ops:
  0.6 43.0 %shard_map.93.reduced = f32[464,128]{1,0:T(8,128)} custom-call(bf16[8,16,14848]{2,1,0:T(8,128)(2,1)} %bitcast.9, bf16[1,14848]{1,0:T(2,128)(2,1)} %bitcast.13, bf16[1,1856]{1,0:T(2,128)(2,1)} %flat_two_ref.1), custom_call_target="tpu_custom_call" | custom-call | tf_op jit(solution)/shard_map/pallas_call | solution.py:396
  43.6 2.1 %shard_map.94 = (f32[464,128]{1,0:T(8,128)}, f32[464,128]{1,0:T(8,128)}, f32[464,128]{1,0:T(8,128)}, f32[464,128]{1,0:T(8,128)}) custom-call(f32[464,128]{1,0:T(8,128)} %shard_map.93.reduced, f32[464,128]{1,0:T(8,128)} %bitcast.10, f32[464,128]{1,0:T(8,128)} %bitcast.11, f32[464,128]{1,0:T(8,128)} %bitcast.12), custom_call_target="tpu_custom_call" | custom-call | flops 950272 | bytes 1900544 | tf_op jit(solution)/shard_map/pallas_call | solution.py:428
